TPU v7x, 32 devices: a whole 2x2x4 slice. The times are simulated.
32 devices in a mesh: dp: 4 (over x, core), fsdp: 8 (over z, y).
Axes of the slice: x: 2, y: 2, z: 4, core: 2. Of those that a mesh axis runs over, the one named last changes fastest.
Arguments:
- gradients: bfloat16 [4, 3072, 2048], P('dp', 'fsdp'), may hold values from -6 to 6
- master: float32 [3072, 2048], P('fsdp', 'dp'), may hold values from -1.3 to 1.3
- moment_one: float32 [3072, 2048], P('fsdp', 'dp'), may hold values from -4 to 4
- moment_two: float32 [3072, 2048], P('fsdp', 'dp'), may hold values from 0.01 to 0.1
- synced: bfloat16 [3072, 2048], P('fsdp', 'dp'), may hold values from -0.75 to 0.75
- rollout: bfloat16 [3072, 2048], P('fsdp', 'dp'), may hold values from -0.77 to 0.77
- amax_record: float32 [24, 16], P('fsdp', 'dp'), may hold values from 0.04 to 1.5
- row_table: int32 [128], replicated, may hold values from 0 to 7, as said below
- expert_owner: int32 [1], replicated, may hold values from 0 to 7
Outputs:
- new_master: float32 [3072, 2048], P('fsdp', 'dp')
- new_one: float32 [3072, 2048], P('fsdp', 'dp')
- new_two: float32 [3072, 2048], P('fsdp', 'dp')
- new_amax: float32 [24, 16], P('fsdp', 'dp')
- new_rollout: bfloat16 [3072, 2048], P('fsdp', 'dp')
Inputs may be any that keep to these rules, and one draw needn't show every extreme that they name: `row_table`: each of 0..7 appears exactly 16 times.
All inputs are finite; a program needn't handle non-finite values.
Results may differ from a plain program's by a relative error of at most 0.014.
Values may be sent and summed in bfloat16 or wider, within the bound.
A program may use at most 64 MiB of HBM per device.

v0:
```python
import jax
import jax.numpy as jnp
from jax import lax
from jax.sharding import PartitionSpec as P

D = 7168
TILE = 128


beta_one = 0.9
beta_two = 0.95
bias_one = 1.0 - 0.9**10
bias_two = 1.0 - 0.95**10
step_size = 0.05
weight_decay = 0.1
adam_floor = 1e-08
code_limit = 448.0


def adam_step(master, moment_one, moment_two, gradient):
    new_one = beta_one * moment_one + (1.0 - beta_one) * gradient
    new_two = beta_two * moment_two + (1.0 - beta_two) * gradient * gradient
    update = new_one / bias_one / (jnp.sqrt(new_two / bias_two) + adam_floor)
    new_master = master - step_size * (update + weight_decay * master)
    return (new_master, new_one, new_two)


def owner_rows(row_table, expert_owner, blocks, owner_count):
    per_owner = TILE // owner_count
    ordering = jnp.argsort(row_table, stable=True)
    experts = blocks * TILE // D
    shifts = expert_owner[experts]
    owners = jnp.arange(owner_count, dtype=jnp.int32)
    first_slot = (owners[None, :] - shifts[:, None]) % owner_count * per_owner
    return ordering[first_slot[:, :, None] + jnp.arange(per_owner, dtype=jnp.int32)[None, None, :]]


def body(
    gradients, master, moment_one, moment_two, synced, rollout, amax_record, row_table, expert_owner
):
    owner_count = lax.axis_size("fsdp")
    replica_count = lax.axis_size("dp")
    row_count, column_count = master.shape
    summed = lax.psum_scatter(
        gradients[0].astype(jnp.float32).astype(jnp.bfloat16), "dp", scatter_dimension=1, tiled=True
    ).astype(jnp.float32)
    new_master, new_one, new_two = adam_step(master, moment_one, moment_two, summed / replica_count)
    difference = new_master - synced.astype(jnp.float32)
    block_count = row_count // TILE
    tile_count = column_count // TILE
    tiled_delta = difference.reshape(block_count, TILE, tile_count, TILE)
    new_amax = jnp.max(jnp.abs(tiled_delta), axis=(1, 3))
    scales = amax_record / code_limit
    code_values = (
        jnp.clip(tiled_delta / scales[:, None, :, None], -code_limit, code_limit)
        .astype(jnp.bfloat16)
        .reshape(block_count, TILE, column_count)
    )
    blocks = lax.axis_index("fsdp") * block_count + jnp.arange(block_count, dtype=jnp.int32)
    chosen = owner_rows(row_table, expert_owner, blocks, owner_count)
    per_owner = TILE // owner_count
    ordered = code_values[jnp.arange(block_count, dtype=jnp.int32)[:, None, None], chosen]
    outgoing = jnp.transpose(ordered, (1, 0, 2, 3)).reshape(
        owner_count, block_count * per_owner, column_count
    )
    spread = jnp.broadcast_to(scales[None], (owner_count, block_count, tile_count))
    incoming, scales_in = (
        lax.all_to_all(outgoing, "fsdp", split_axis=0, concat_axis=0, tiled=True),
        lax.all_to_all(
            spread.astype(jnp.bfloat16), "fsdp", split_axis=0, concat_axis=0, tiled=True
        ).astype(spread.dtype),
    )
    restored = (
        incoming.reshape(owner_count, block_count, per_owner, tile_count, TILE).astype(jnp.float32)
        * scales_in[:, :, None, :, None]
    )
    new_rollout = (rollout.astype(jnp.float32) + restored.reshape(row_count, column_count)).astype(
        jnp.bfloat16
    )
    return (new_master, new_one, new_two, new_amax, new_rollout)


def solution(mesh):
    return jax.shard_map(
        body,
        mesh=mesh,
        in_specs=(
            P("dp", "fsdp", None),
            P("fsdp", "dp"),
            P("fsdp", "dp"),
            P("fsdp", "dp"),
            P("fsdp", "dp"),
            P("fsdp", "dp"),
            P("fsdp", "dp"),
            P(),
            P(),
        ),
        out_specs=(
            P("fsdp", "dp"),
            P("fsdp", "dp"),
            P("fsdp", "dp"),
            P("fsdp", "dp"),
            P("fsdp", "dp"),
        ),
        check_vma=False,
    )
```

profile of v0, /device:TPU:0, one launch (start us, length us, event | category | flops | bytes accessed | tf_op | source)
XLA Modules:
  0.0 75.3 jit_solution(50823773335896001)
XLA Ops:
  7.2 0.0 copy-start.5
  7.2 0.0 copy-start.6
  7.2 0.0 reduce-scatter.2.cloned.1.call-start
  7.2 0.7 reduce-scatter.2.cloned.1.call-update
  7.9 0.0 copy-done.5
  7.9 0.6 broadcast_in_dim.5
  8.5 7.3 %all-to-all-start.1 = ((bf16[8,3,4]{2,1,0:T(4,128)(2,1)}), bf16[8,3,4]{2,1,0:T(4,128)(2,1)}, u32[]{:S(2)}, u32[]{:S(2)}) async-start(bf16[8,3,4]{2,1,0:T(4,128)(2,1)} %broadcast_in_dim.5), calls=%async_computation.2 | async-start | bytes 16384 | tf_op jit(solution)/shard_map/all_to_all | solution.py:69
  15.8 0.1 broadcast_bitcast_fusion
  16.6 0.1 compare_select_fusion.1
  16.6 0.1 reshape.87
  16.7 0.0 copy-done.6
  16.7 2.5 %sort.17 = (s32[128]{0:T(128)}, s32[128]{0:T(128)S(1)}) sort(s32[128]{0:T(128)S(1)} %copy-done.6, s32[128]{0:T(128)S(1)} %iota.21), dimensions={0}, to_apply=%region_2.3 | sort | flops 896 | bytes 2048 | tf_op jit(solution)/shard_map/jit(argsort)/sort | solution.py:30
  19.3 0.0 copy-start.2
  19.3 0.0 copy-start.3
  19.3 2.7 %gather_fusion = s32[384]{0:T(512)S(1)} fusion(s32[128]{0:T(128)S(1)} %get-tuple-element.6, s32[1024]{0:T(1024)S(1)} %pad_clamp_fusion), kind=kCustom, calls=%fused_computation | custom fusion | bytes 4608 | tf_op jit(solution)/shard_map/gather | solution.py:35
  22.0 0.1 gather.10
  22.1 0.1 reshape.93
  22.2 19.5 %reduce-scatter.2.cloned.1.call-done = bf16[384,512]{1,0:T(8,128)(2,1)} async-done(((bf16[384,2048]{1,0:T(8,128)(2,1)}), bf16[384,512]{1,0:T(8,128)(2,1)}) %reduce-scatter.2.cloned.1.call-update) | async-done | bytes 393232 | tf_op jit(solution)/shard_map/reduce_scatter | solution.py:44
  41.7 0.0 copy-done
  41.7 0.0 copy-done.3
  41.7 2.9 %fusion.11 = (f32[384,512]{1,0:T(8,128)S(1)}, f32[384,512]{1,0:T(8,128)S(1)}, f32[384,512]{1,0:T(8,128)}, f32[384,512]{1,0:T(8,128)}, f32[384,512]{1,0:T(8,128)}) fusion(bf16[384,512]{1,0:T(8,128)(2,1)S(1)} %copy-done.3, f32[384,512]{1,0:T(8,128)S(1)} %copy-done, bf16[384,512]{1,0:T(8,128)(2,1)} %reduce-scatter.2.cloned.1.call-done, ...), kind=kLoop, calls=%fused_computation.29 | loop fusion | flops 3932160 | bytes 7077888 | tf_op jit(solution)/shard_map/abs | solution.py:52
  44.6 0.1 clamp_convert_fusion
  44.7 3.9 %gather_fusion.1 = bf16[384,512]{1,0:T(8,128)(2,1)S(1)} fusion(bf16[3,128,512]{2,1,0:T(8,128)(2,1)S(1)} %clamp_convert_fusion, s32[384]{0:T(512)S(1)} %reshape.93), kind=kCustom, calls=%fused_computation.1 | custom fusion | bytes 789504 | tf_op jit(solution)/shard_map/gather | solution.py:62
  48.6 0.8 %copy.14 = bf16[3,8,16,512]{3,2,0,1:T(8,128)(2,1)} copy(bf16[3,8,16,512]{3,2,1,0:T(8,128)(2,1)S(1)} %bitcast.35) | data formatting | bytes 786432 | tf_op jit(solution)/shard_map/gather | solution.py:62
  49.4 0.0 all-to-all-done.1
  49.4 5.5 %all-to-all-start = ((bf16[8,48,512]{2,1,0:T(8,128)(2,1)}), bf16[8,48,512]{2,1,0:T(8,128)(2,1)S(1)}, u32[]{:S(2)}, u32[]{:S(2)}) async-start(bf16[8,48,512]{2,1,0:T(8,128)(2,1)} %bitcast.5), calls=%async_computation.1 | async-start | bytes 786432 | tf_op jit(solution)/shard_map/all_to_all | solution.py:68
  54.9 0.3 abs.7
  55.2 0.8 %reduce_max.9 = f32[3,4]{1,0:T(4,128)} reduce(f32[3,128,4,128]{3,2,1,0:T(4,128)S(1)} %abs.7, f32[]{:T(128)} %constant.30.clone.1), dimensions={1,3}, to_apply=%region_1.0 | reduce | flops 196596 | bytes 786484 | tf_op jit(solution)/shard_map/reduce_max | solution.py:52
  56.0 10.6 %all-to-all-done = bf16[8,48,512]{2,1,0:T(8,128)(2,1)S(1)} async-done(((bf16[8,48,512]{2,1,0:T(8,128)(2,1)}), bf16[8,48,512]{2,1,0:T(8,128)(2,1)S(1)}, u32[]{:S(2)}, u32[]{:S(2)}) %all-to-all-start) | async-done | bytes 393248 | tf_op jit(solution)/shard_map/all_to_all | solution.py:68
  66.6 0.9 %mul.63 = f32[8,3,16,4,128]{4,3,2,1,0:T(4,128)S(1)} broadcast(bf16[8,3,4]{2,1,0:T(4,128)(2,1)} %all-to-all-done.1), dimensions={0,1,3} | broadcast | bytes 786624 | tf_op jit(solution)/shard_map/mul | solution.py:74
  67.5 0.0 copy-done.4
  67.5 1.0 %fusion.4 = bf16[384,512]{1,0:T(8,128)(2,1)} fusion(f32[48,8,4,128]{3,2,1,0:T(4,128)S(1)} %bitcast.33, bf16[384,512]{1,0:T(8,128)(2,1)S(1)} %copy-done.4, bf16[8,48,512]{2,1,0:T(8,128)(2,1)S(1)} %all-to-all-done), kind=kLoop, calls=%fused_computation.10 | loop fusion | flops 983040 | bytes 1966080 | tf_op jit(solution)/shard_map/convert_element_type | solution.py:77
  (11 shorter events, 0.1 us)
Async XLA Ops:
  7.2 0.8 %copy-start.5 = (f32[3,4]{1,0:T(4,128)S(1)}, f32[3,4]{1,0:T(4,128)}, u32[]{:S(2)}) copy-start(f32[3,4]{1,0:T(4,128)} %param.15) | copy-start | bytes 148
  7.2 9.5 %copy-start.6 = (s32[128]{0:T(128)S(1)}, s32[128]{0:T(128)}, u32[]{:S(2)}) copy-start(s32[128]{0:T(128)} %param.16) | copy-start | bytes 1540
  7.2 34.5 %reduce-scatter.2.cloned.1.call-start = ((), (), s32[]{:S(2)}) async-start(), calls=%async_computation.3 | async-start | bytes 1966080 | tf_op jit(solution)/shard_map/reduce_scatter | solution.py:44
  8.5 40.9 %all-to-all-start.1 = ((bf16[8,3,4]{2,1,0:T(4,128)(2,1)}), bf16[8,3,4]{2,1,0:T(4,128)(2,1)}, u32[]{:S(2)}, u32[]{:S(2)}) async-start(bf16[8,3,4]{2,1,0:T(4,128)(2,1)} %broadcast_in_dim.5), calls=%async_computation.2 | async-start | bytes 16384 | tf_op jit(solution)/shard_map/all_to_all | solution.py:69
  19.3 22.4 %copy-start = (f32[384,512]{1,0:T(8,128)S(1)}, f32[384,512]{1,0:T(8,128)}, u32[]{:S(2)}) copy-start(f32[384,512]{1,0:T(8,128)} %param.10) | copy-start | bytes 2359300
  19.3 22.4 %copy-start.1 = (f32[384,512]{1,0:T(8,128)S(1)}, f32[384,512]{1,0:T(8,128)}, u32[]{:S(2)}) copy-start(f32[384,512]{1,0:T(8,128)} %param.11) | copy-start | bytes 2359300
  19.3 22.4 %copy-start.2 = (f32[384,512]{1,0:T(8,128)S(1)}, f32[384,512]{1,0:T(8,128)}, u32[]{:S(2)}) copy-start(f32[384,512]{1,0:T(8,128)} %param.12) | copy-start | bytes 2359300
  19.3 22.4 %copy-start.3 = (bf16[384,512]{1,0:T(8,128)(2,1)S(1)}, bf16[384,512]{1,0:T(8,128)(2,1)}, u32[]{:S(2)}) copy-start(bf16[384,512]{1,0:T(8,128)(2,1)} %param.13) | copy-start | bytes 1179652
  49.4 17.2 %all-to-all-start = ((bf16[8,48,512]{2,1,0:T(8,128)(2,1)}), bf16[8,48,512]{2,1,0:T(8,128)(2,1)S(1)}, u32[]{:S(2)}, u32[]{:S(2)}) async-start(bf16[8,48,512]{2,1,0:T(8,128)(2,1)} %bitcast.5), calls=%async_computation.1 | async-start | bytes 786432 | tf_op jit(solution)/shard_map/all_to_all | solution.py:68
  54.9 12.6 %copy-start.4 = (bf16[384,512]{1,0:T(8,128)(2,1)S(1)}, bf16[384,512]{1,0:T(8,128)(2,1)}, u32[]{:S(2)}) copy-start(bf16[384,512]{1,0:T(8,128)(2,1)} %param.14) | copy-start | bytes 1179652
Sparse Core Ops, SparseCore 0:
  10.6 31.0 reduce-scatter.1
where the time goes:
time: 75.6 us; the launch traced here: 75.3 us
  waiting for transfers between devices  30.8 us (41%)
  between operations  14.8 us (20%)
  starting transfers between devices  12.8 us (17%)
  local copies, waits for them, and re-layouts  9.43 us (12%)
  other arithmetic  7.44 us (10%)
    reduce_scatter x1, waiting for transfers between devices, body(): lax.psum_scatter(gradients[0].astype(jnp.float32).astype(jnp.bfloat16), '...  19.5 us
    all_to_all x1, waiting for transfers between devices, body(): lax.all_to_all(outgoing, 'fsdp', split_axis=0, concat_axis=0, tiled=True)  10.6 us
    all_to_all x1, starting transfers between devices, body(): lax.all_to_all(spread.astype(jnp.bfloat16), 'fsdp', split_axis=0, concat_...  7.28 us
    all_to_all x1, starting transfers between devices, body(): lax.all_to_all(outgoing, 'fsdp', split_axis=0, concat_axis=0, tiled=True)  5.52 us
    gather x2, local copies, waits for them, and re-layouts, body(): code_values[jnp.arange(block_count, dtype=jnp.int32)[:, None, None], chosen]  4.67 us
    abs x1, other arithmetic, body(): new_amax = jnp.max(jnp.abs(tiled_delta), axis=(1, 3))  2.91 us
    gather x2, local copies, waits for them, and re-layouts, owner_rows(): ordering[first_slot[:, :, None] + jnp.arange(per_owner, dtype=jnp.int32)[...  2.77 us
    sort x1, other arithmetic, owner_rows(): ordering = jnp.argsort(row_table, stable=True)  2.54 us
  transfers between devices with their start and end apart: 3, of which 2 were waited for; matrix products, arithmetic and copies ran while one was open for 20% of the time, Pallas kernels for 0%

commit v1 on v0

--- a/solution.py
+++ b/solution.py
@@ -1,11 +1,15 @@
+import functools
+
 import jax
 import jax.numpy as jnp
 from jax import lax
+from jax.experimental import pallas as pl
+from jax.experimental.pallas import tpu as pltpu
 from jax.sharding import PartitionSpec as P
 
 D = 7168
 TILE = 128
-
+MESH = pl.DeviceIdType.MESH
 
 beta_one = 0.9
 beta_two = 0.95
@@ -25,6 +29,237 @@
     return (new_master, new_one, new_two)
 
 
+HALVES = 2
+
+
+def flipped(index, mask):
+    out = index
+    bit = 1
+    while bit <= mask:
+        if mask & bit:
+            out = out + bit - 2 * bit * (lax.rem(index // bit, 2))
+        bit *= 2
+    return out
+
+
+def fused_kernel(
+    owners, grads, master, one, two, synced, rollout, amax, table, shifts,
+    master_out, one_out, two_out, amax_out, rollout_out,
+    far_own, near_own, far_sib, near_sib, far_sum, far_in,
+    master_v, one_v, two_v, synced_v, rollout_v,
+    master_w, one_w, two_w, rollout_w, packed, arrived,
+    load_sem, far_send, far_recv, near_send, near_recv, x_send, x_recv, row_send, row_recv, store_sem,
+):
+    d = lax.axis_index("dp")
+    f = lax.axis_index("fsdp")
+    rows, cols = master_v.shape
+    blocks = rows // TILE
+    width = cols // HALVES
+    part = TILE // owners
+    chunks = [(b, h) for b in range(blocks) for h in range(HALVES)]
+    sib = flipped(d, 1)
+    opp = flipped(d, 2)
+    opp_sib = flipped(d, 3)
+
+    barrier = pltpu.get_barrier_semaphore()
+    pl.semaphore_signal(barrier, inc=1, device_id={"dp": sib}, device_id_type=MESH)
+    pl.semaphore_signal(barrier, inc=1, device_id={"dp": opp}, device_id_type=MESH)
+    for j in range(1, owners):
+        pl.semaphore_signal(barrier, inc=1, device_id={"fsdp": flipped(f, j)}, device_id_type=MESH)
+
+    def columns(q):
+        return pl.ds(pl.multiple_of(q * cols, cols), cols)
+
+    loads = [
+        pltpu.make_async_copy(src, dst, load_sem.at[n])
+        for n, (src, dst) in enumerate([
+            (grads.at[:, columns(opp)], far_own),
+            (grads.at[:, columns(d)], near_own),
+            (one, one_v),
+            (two, two_v),
+            (master, master_v),
+            (synced, synced_v),
+            (rollout, rollout_v),
+        ])
+    ]
+    for load in loads:
+        load.start()
+
+    ti = lax.broadcasted_iota(jnp.int32, (TILE, TILE), 0)
+    tj = lax.broadcasted_iota(jnp.int32, (TILE, TILE), 1)
+    key_row = table[...] * TILE + lax.broadcasted_iota(jnp.int32, (1, TILE), 1)
+    key_mat = jnp.broadcast_to(key_row, (TILE, TILE)).astype(jnp.float32)
+    key_col = jnp.sum(jnp.where(ti == tj, key_mat, 0.0), axis=1, keepdims=True)
+    rank = jnp.sum(jnp.where(key_col < key_mat, 1.0, 0.0), axis=0, keepdims=True).astype(jnp.int32)
+
+    def chooser(b):
+        shift = shifts[((f * blocks + b) * TILE) // D]
+        dest = (rank + shift * part) & (TILE - 1)
+        return jnp.where(ti == dest, 1.0, 0.0).astype(jnp.bfloat16)
+
+    pl.semaphore_wait(barrier, owners + 1)
+
+    def at(ref, b, h):
+        return ref.at[pl.ds(b * TILE, TILE), pl.ds(h * width, width)]
+
+    far_copies = []
+    for n, (b, h) in enumerate(chunks):
+        source = pl.multiple_of(opp_sib * cols + h * width, width)
+        copy = pltpu.make_async_remote_copy(
+            src_ref=grads.at[pl.ds(b * TILE, TILE), pl.ds(source, width)],
+            dst_ref=at(far_sib, b, h),
+            send_sem=far_send.at[n], recv_sem=far_recv.at[n],
+            device_id={"dp": sib}, device_id_type=MESH,
+        )
+        copy.start()
+        far_copies.append(copy)
+    near_copies = []
+    for b in range(blocks):
+        copy = pltpu.make_async_remote_copy(
+            src_ref=grads.at[pl.ds(b * TILE, TILE), columns(sib)],
+            dst_ref=near_sib.at[pl.ds(b * TILE, TILE), :],
+            send_sem=near_send.at[b], recv_sem=near_recv.at[b],
+            device_id={"dp": sib}, device_id_type=MESH,
+        )
+        copy.start()
+        near_copies.append(copy)
+
+    x_copies = []
+    loads[0].wait()
+    for n, (b, h) in enumerate(chunks):
+        far_copies[n].wait_recv()
+        mine = at(far_own, b, h)[...].astype(jnp.float32)
+        theirs = at(far_sib, b, h)[...].astype(jnp.float32)
+        at(far_sum, b, h)[...] = (mine + theirs).astype(jnp.bfloat16)
+        copy = pltpu.make_async_remote_copy(
+            src_ref=at(far_sum, b, h), dst_ref=at(far_in, b, h),
+            send_sem=x_send.at[n], recv_sem=x_recv.at[n],
+            device_id={"dp": opp}, device_id_type=MESH,
+        )
+        copy.start()
+        x_copies.append(copy)
+
+    for load in loads[1:]:
+        load.wait()
+
+    row_copies = []
+    stores = []
+    choose = None
+    for n, (b, h) in enumerate(chunks):
+        if h == 0:
+            near_copies[b].wait_recv()
+            choose = chooser(b)
+        x_copies[n].wait_recv()
+        summed = (
+            at(near_own, b, h)[...].astype(jnp.float32)
+            + at(near_sib, b, h)[...].astype(jnp.float32)
+            + at(far_in, b, h)[...].astype(jnp.float32)
+        )
+        new_master, new_one, new_two = adam_step(
+            at(master_v, b, h)[...], at(one_v, b, h)[...], at(two_v, b, h)[...], summed / 4.0
+        )
+        at(master_w, b, h)[...] = new_master
+        at(one_w, b, h)[...] = new_one
+        at(two_w, b, h)[...] = new_two
+        delta = new_master - at(synced_v, b, h)[...].astype(jnp.float32)
+        restored = []
+        for k in range(width // TILE):
+            t = h * (width // TILE) + k
+            piece = delta[:, k * TILE : (k + 1) * TILE]
+            top = jnp.max(jnp.max(jnp.abs(piece), axis=0, keepdims=True), axis=1, keepdims=True)
+            amax_out[b : b + 1, t : t + 1] = top
+            limit = amax[b, t] / code_limit * code_limit
+            restored.append(jnp.clip(piece, -limit, limit).astype(jnp.bfloat16))
+        restored = jnp.concatenate(restored, axis=1)
+        packed[b, :, pl.ds(h * width, width)] = jnp.dot(
+            choose, restored, preferred_element_type=jnp.float32
+        ).astype(jnp.bfloat16)
+        for j in sorted(range(1, owners), key=lambda j: -(j // 2)):
+            target = flipped(f, j)
+            copy = pltpu.make_async_remote_copy(
+                src_ref=packed.at[b, pl.ds(pl.multiple_of(target * part, part), part), pl.ds(h * width, width)],
+                dst_ref=arrived.at[f, b, :, pl.ds(h * width, width)],
+                send_sem=row_send.at[n, j - 1], recv_sem=row_recv.at[n, j - 1],
+                device_id={"fsdp": target}, device_id_type=MESH,
+            )
+            copy.start()
+            row_copies.append((n, copy))
+        arrived[f, b, :, pl.ds(h * width, width)] = packed[
+            b, pl.ds(pl.multiple_of(f * part, part), part), pl.ds(h * width, width)
+        ]
+        if h == HALVES - 1:
+            for m, (src, dst) in enumerate([(master_w, master_out), (one_w, one_out), (two_w, two_out)]):
+                cut = pl.ds(b * TILE, TILE)
+                store = pltpu.make_async_copy(src.at[cut, :], dst.at[cut, :], store_sem.at[m * blocks + b])
+                store.start()
+                stores.append(store)
+
+    for n, (b, h) in enumerate(chunks):
+        for m, copy in row_copies:
+            if m == n:
+                copy.wait_recv()
+        cut = pl.ds(h * width, width)
+        rollout_w[:, b, :, cut] = (
+            rollout_v[:, b, :, cut].astype(jnp.float32) + arrived[:, b, :, cut].astype(jnp.float32)
+        ).astype(jnp.bfloat16)
+        if h == HALVES - 1:
+            store = pltpu.make_async_copy(
+                rollout_w.at[:, b], rollout_out.at[:, b], store_sem.at[3 * blocks + b]
+            )
+            store.start()
+            stores.append(store)
+
+    for copy in far_copies + near_copies + x_copies + [c for _, c in row_copies]:
+        copy.wait_send()
+    for store in stores:
+        store.wait()
+
+
+def fused_body(gradients, master, one, two, synced, rollout, amax, table, shifts):
+    owners = lax.axis_size("fsdp")
+    rows, cols = master.shape
+    blocks = rows // TILE
+    part = TILE // owners
+    n = blocks * HALVES
+    f32, bf16 = jnp.float32, jnp.bfloat16
+    hbm = pl.BlockSpec(memory_space=pl.ANY)
+    vmem = pl.BlockSpec(memory_space=pltpu.VMEM)
+    smem = pl.BlockSpec(memory_space=pltpu.SMEM)
+    grouped = (owners, blocks, part, cols)
+    whole = (rows, cols)
+    dma = pltpu.SemaphoreType.DMA
+    outs = pl.pallas_call(
+        functools.partial(fused_kernel, owners),
+        out_shape=(
+            jax.ShapeDtypeStruct(whole, f32),
+            jax.ShapeDtypeStruct(whole, f32),
+            jax.ShapeDtypeStruct(whole, f32),
+            jax.ShapeDtypeStruct(amax.shape, f32),
+            jax.ShapeDtypeStruct(grouped, bf16),
+        ),
+        in_specs=[hbm] * 6 + [smem, vmem, smem],
+        out_specs=(hbm, hbm, hbm, vmem, hbm),
+        scratch_shapes=(
+            [pltpu.VMEM(whole, bf16)] * 6
+            + [pltpu.VMEM(whole, f32)] * 3
+            + [pltpu.VMEM(whole, bf16), pltpu.VMEM(grouped, bf16)]
+            + [pltpu.VMEM(whole, f32)] * 3
+            + [pltpu.VMEM(grouped, bf16), pltpu.VMEM((blocks, TILE, cols), bf16), pltpu.VMEM(grouped, bf16)]
+            + [
+                dma((7,)), dma((n,)), dma((n,)), dma((blocks,)), dma((blocks,)), dma((n,)), dma((n,)),
+                dma((n, owners - 1)), dma((n, owners - 1)), dma((4 * blocks,)),
+            ]
+        ),
+        compiler_params=pltpu.CompilerParams(
+            collective_id=0, has_side_effects=True, vmem_limit_bytes=32 * 1024 * 1024
+        ),
+    )(
+        gradients[0], master, one, two, synced, rollout.reshape(grouped), amax,
+        table.reshape(1, TILE), shifts,
+    )
+    return outs[0], outs[1], outs[2], outs[3], outs[4].reshape(whole)
+
+
 def owner_rows(row_table, expert_owner, blocks, owner_count):
     per_owner = TILE // owner_count
     ordering = jnp.argsort(row_table, stable=True)
@@ -35,7 +270,7 @@
     return ordering[first_slot[:, :, None] + jnp.arange(per_owner, dtype=jnp.int32)[None, None, :]]
 
 
-def body(
+def plain_body(
     gradients, master, moment_one, moment_two, synced, rollout, amax_record, row_table, expert_owner
 ):
     owner_count = lax.axis_size("fsdp")
@@ -81,8 +316,10 @@
 
 
 def solution(mesh):
+    sizes = dict(mesh.shape)
+    fits = sizes["dp"] == 4 and sizes["fsdp"] == 8
     return jax.shard_map(
-        body,
+        fused_body if fits else plain_body,
         mesh=mesh,
         in_specs=(
             P("dp", "fsdp", None),

time: 75.6 us -> 37 us (0.49)
  waiting for transfers between devices: 30.8 us -> 0 us
  Pallas kernels: 0 us -> 23.3 us
  between operations: 14.8 us -> 1.31 us
  starting transfers between devices: 12.8 us -> 0 us
  other arithmetic: 7.44 us -> 0 us
  local copies, waits for them, and re-layouts: 9.43 us -> 12.1 us
    pallas_call x0 -> x1, Pallas kernels: none -> 23.3 us  [fused_body(): pl.pallas_call(functools.partial(fused_kernel, owners), out_shape=(jax.Sh...]
    reduce_scatter x1 -> x0, waiting for transfers between devices: 19.5 us -> none  [body(): lax.psum_scatter(gradients[0].astype(jnp.float32).astype(jnp.bfloat16), '...]
    all_to_all x2 -> x0, starting transfers between devices: 12.8 us -> none  [the longest x1 7.28 us: body(): lax.all_to_all(spread.astype(jnp.bfloat16), 'fsdp', split_axis=0, concat_...]
    unnamed x16 -> x21, local copies, waits for them, and re-layouts: 0.11 us -> 12.1 us
    all_to_all x2 -> x0, waiting for transfers between devices: 10.6 us -> none  [the longest x1 10.6 us: body(): lax.all_to_all(outgoing, 'fsdp', split_axis=0, concat_axis=0, tiled=True)]
    gather x4 -> x0, local copies, waits for them, and re-layouts: 7.43 us -> none  [the longest x2 4.67 us: body(): code_values[jnp.arange(block_count, dtype=jnp.int32)[:, None, None], chosen]]
    abs x1 -> x0, other arithmetic: 2.91 us -> none  [body(): new_amax = jnp.max(jnp.abs(tiled_delta), axis=(1, 3))]
    sort x1 -> x0, other arithmetic: 2.54 us -> none  [owner_rows(): ordering = jnp.argsort(row_table, stable=True)]
  transfers between devices with their start and end apart: 3 -> 0, of which waited for: 2 -> 0; matrix products, arithmetic and copies ran while one was open for 20% -> 0% of each run, Pallas kernels for 0% -> 0%
where the time goes in v1:
time: 37 us; the launch traced here: 36.6 us
  Pallas kernels  23.3 us (63%)
  local copies, waits for them, and re-layouts  12.1 us (33%)
  between operations  1.31 us (4%)
    pallas_call x1, Pallas kernels, fused_body(): pl.pallas_call(functools.partial(fused_kernel, owners), out_shape=(jax.Sh...  23.3 us
    unnamed x21, local copies, waits for them, and re-layouts  12.1 us

profile of v1, /device:TPU:0, one launch (start us, length us, event | category | flops | bytes accessed | tf_op | source)
XLA Modules:
  0.0 36.6 jit_solution(13696591474740672922)
XLA Ops:
  1.3 0.0 copy-start
  1.3 1.4 %copy-done = bf16[1,384,2048]{2,1,0:T(8,128)(2,1)S(1)} copy-done((bf16[1,384,2048]{2,1,0:T(8,128)(2,1)S(1)}, bf16[1,384,2048]{2,1,0:T(8,128)(2,1)}, u32[]{:S(2)}) %copy-start) | copy-done | bytes 1572888
  2.7 0.0 copy-start.1
  2.7 1.1 %copy-done.1 = f32[384,512]{1,0:T(8,128)S(1)} copy-done((f32[384,512]{1,0:T(8,128)S(1)}, f32[384,512]{1,0:T(8,128)}, u32[]{:S(2)}) %copy-start.1) | copy-done | bytes 786456
  3.8 0.0 copy-start.2
  3.8 1.1 %copy-done.2 = f32[384,512]{1,0:T(8,128)S(1)} copy-done((f32[384,512]{1,0:T(8,128)S(1)}, f32[384,512]{1,0:T(8,128)}, u32[]{:S(2)}) %copy-start.2) | copy-done | bytes 786456
  5.0 0.0 copy-start.3
  5.0 1.1 %copy-done.3 = f32[384,512]{1,0:T(8,128)S(1)} copy-done((f32[384,512]{1,0:T(8,128)S(1)}, f32[384,512]{1,0:T(8,128)}, u32[]{:S(2)}) %copy-start.3) | copy-done | bytes 786456
  6.1 0.0 copy-start.4
  6.1 1.0 %copy-done.4 = bf16[384,512]{1,0:T(8,128)(2,1)S(1)} copy-done((bf16[384,512]{1,0:T(8,128)(2,1)S(1)}, bf16[384,512]{1,0:T(8,128)(2,1)}, u32[]{:S(2)}) %copy-start.4) | copy-done | bytes 393240
  7.1 0.0 copy-start.5
  7.1 1.0 %copy-done.5 = bf16[384,512]{1,0:T(8,128)(2,1)S(1)} copy-done((bf16[384,512]{1,0:T(8,128)(2,1)S(1)}, bf16[384,512]{1,0:T(8,128)(2,1)}, u32[]{:S(2)}) %copy-start.5) | copy-done | bytes 393240
  8.1 0.0 copy-start.6
  8.1 0.7 %copy-done.6 = f32[3,4]{1,0:T(4,128)S(1)} copy-done((f32[3,4]{1,0:T(4,128)S(1)}, f32[3,4]{1,0:T(4,128)}, u32[]{:S(2)}) %copy-start.6) | copy-done | bytes 72
  8.8 0.0 copy-start.7
  8.8 0.7 %copy-done.7 = s32[128]{0:T(128)S(1)} copy-done((s32[128]{0:T(128)S(1)}, s32[128]{0:T(128)}, u32[]{:S(2)}) %copy-start.7) | copy-done | bytes 536
  9.4 23.3 %shard_map.128 = (f32[384,512]{1,0:T(8,128)S(1)}, f32[384,512]{1,0:T(8,128)S(1)}, f32[384,512]{1,0:T(8,128)S(1)}, f32[3,4]{1,0:T(4,128)S(1)}, bf16[8,3,16,512]{3,2,1,0:T(8,128)(2,1)S(1)}) custom-call(bf16[384,2048]{1,0:T(8,128)(2,1)S(1)} %bitcast.4, f32[384,512]{1,0:T(8,128)S(1)} %copy-done.1, f32[384,512]{1,0:T(8,128)S(1)} %copy-done.2, ...), custom_call_target="tpu_custom_call" | custom-call | tf_op jit(solution)/shard_map/pallas_call | solution.py:231
  32.7 0.9 %copy.20 = f32[384,512]{1,0:T(8,128)} copy(f32[384,512]{1,0:T(8,128)S(1)} %get-tuple-element.20) | data formatting | bytes 1572864
  33.6 0.9 %copy.21 = f32[384,512]{1,0:T(8,128)} copy(f32[384,512]{1,0:T(8,128)S(1)} %get-tuple-element.21) | data formatting | bytes 1572864
  34.4 0.9 %copy.22 = f32[384,512]{1,0:T(8,128)} copy(f32[384,512]{1,0:T(8,128)S(1)} %get-tuple-element.22) | data formatting | bytes 1572864
  35.3 0.6 %copy.23 = f32[3,4]{1,0:T(4,128)} copy(f32[3,4]{1,0:T(4,128)S(1)} %get-tuple-element.23) | data formatting | bytes 96
  35.9 0.7 %copy.24 = bf16[384,512]{1,0:T(8,128)(2,1)} copy(bf16[384,512]{1,0:T(8,128)(2,1)S(1)} %bitcast.6) | data formatting | bytes 786432
Async XLA Ops:
  1.3 1.4 %copy-start = (bf16[1,384,2048]{2,1,0:T(8,128)(2,1)S(1)}, bf16[1,384,2048]{2,1,0:T(8,128)(2,1)}, u32[]{:S(2)}) copy-start(bf16[1,384,2048]{2,1,0:T(8,128)(2,1)} %param.9) | copy-start | bytes 4718596
  2.7 1.1 %copy-start.1 = (f32[384,512]{1,0:T(8,128)S(1)}, f32[384,512]{1,0:T(8,128)}, u32[]{:S(2)}) copy-start(f32[384,512]{1,0:T(8,128)} %master.1) | copy-start | bytes 2359300
  3.8 1.1 %copy-start.2 = (f32[384,512]{1,0:T(8,128)S(1)}, f32[384,512]{1,0:T(8,128)}, u32[]{:S(2)}) copy-start(f32[384,512]{1,0:T(8,128)} %one.1) | copy-start | bytes 2359300
  5.0 1.1 %copy-start.3 = (f32[384,512]{1,0:T(8,128)S(1)}, f32[384,512]{1,0:T(8,128)}, u32[]{:S(2)}) copy-start(f32[384,512]{1,0:T(8,128)} %two.1) | copy-start | bytes 2359300
  6.1 1.0 %copy-start.4 = (bf16[384,512]{1,0:T(8,128)(2,1)S(1)}, bf16[384,512]{1,0:T(8,128)(2,1)}, u32[]{:S(2)}) copy-start(bf16[384,512]{1,0:T(8,128)(2,1)} %synced.1) | copy-start | bytes 1179652
  7.1 1.0 %copy-start.5 = (bf16[384,512]{1,0:T(8,128)(2,1)S(1)}, bf16[384,512]{1,0:T(8,128)(2,1)}, u32[]{:S(2)}) copy-start(bf16[384,512]{1,0:T(8,128)(2,1)} %param.14) | copy-start | bytes 1179652
  8.1 0.7 %copy-start.6 = (f32[3,4]{1,0:T(4,128)S(1)}, f32[3,4]{1,0:T(4,128)}, u32[]{:S(2)}) copy-start(f32[3,4]{1,0:T(4,128)} %amax.1) | copy-start | bytes 148
  8.8 0.7 %copy-start.7 = (s32[128]{0:T(128)S(1)}, s32[128]{0:T(128)}, u32[]{:S(2)}) copy-start(s32[128]{0:T(128)} %param.16) | copy-start | bytes 1540

commit v2 on v1

--- a/solution.py
+++ b/solution.py
@@ -43,12 +43,11 @@
 
 
 def fused_kernel(
-    owners, grads, master, one, two, synced, rollout, amax, table, shifts,
-    master_out, one_out, two_out, amax_out, rollout_out,
+    owners, grads, master, one, two, synced, rollout, amax_h, table_h, shifts,
+    master_w, one_w, two_w, amax_out, rollout_w,
     far_own, near_own, far_sib, near_sib, far_sum, far_in,
-    master_v, one_v, two_v, synced_v, rollout_v,
-    master_w, one_w, two_w, rollout_w, packed, arrived,
-    load_sem, far_send, far_recv, near_send, near_recv, x_send, x_recv, row_send, row_recv, store_sem,
+    master_v, one_v, two_v, synced_v, rollout_v, packed, arrived, amax, table,
+    load_sem, far_send, far_recv, near_send, near_recv, x_send, x_recv, row_send, row_recv,
 ):
     d = lax.axis_index("dp")
     f = lax.axis_index("fsdp")
@@ -73,6 +72,8 @@
     loads = [
         pltpu.make_async_copy(src, dst, load_sem.at[n])
         for n, (src, dst) in enumerate([
+            (table_h, table),
+            (amax_h, amax),
             (grads.at[:, columns(opp)], far_own),
             (grads.at[:, columns(d)], near_own),
             (one, one_v),
@@ -84,14 +85,6 @@
     ]
     for load in loads:
         load.start()
-
-    ti = lax.broadcasted_iota(jnp.int32, (TILE, TILE), 0)
-    tj = lax.broadcasted_iota(jnp.int32, (TILE, TILE), 1)
-    key_row = table[...] * TILE + lax.broadcasted_iota(jnp.int32, (1, TILE), 1)
-    key_mat = jnp.broadcast_to(key_row, (TILE, TILE)).astype(jnp.float32)
-    key_col = jnp.sum(jnp.where(ti == tj, key_mat, 0.0), axis=1, keepdims=True)
-    rank = jnp.sum(jnp.where(key_col < key_mat, 1.0, 0.0), axis=0, keepdims=True).astype(jnp.int32)
-
     def chooser(b):
         shift = shifts[((f * blocks + b) * TILE) // D]
         dest = (rank + shift * part) & (TILE - 1)
@@ -125,7 +118,7 @@
         near_copies.append(copy)
 
     x_copies = []
-    loads[0].wait()
+    loads[2].wait()
     for n, (b, h) in enumerate(chunks):
         far_copies[n].wait_recv()
         mine = at(far_own, b, h)[...].astype(jnp.float32)
@@ -139,11 +132,19 @@
         copy.start()
         x_copies.append(copy)
 
-    for load in loads[1:]:
+    for load in loads[:2]:
         load.wait()
 
+    ti = lax.broadcasted_iota(jnp.int32, (TILE, TILE), 0)
+    tj = lax.broadcasted_iota(jnp.int32, (TILE, TILE), 1)
+    key_row = table[...] * TILE + lax.broadcasted_iota(jnp.int32, (1, TILE), 1)
+    key_mat = jnp.broadcast_to(key_row, (TILE, TILE)).astype(jnp.float32)
+    key_col = jnp.sum(jnp.where(ti == tj, key_mat, 0.0), axis=1, keepdims=True)
+    rank = jnp.sum(jnp.where(key_col < key_mat, 1.0, 0.0), axis=0, keepdims=True).astype(jnp.int32)
+    for load in loads[3:]:
+        load.wait()
+
     row_copies = []
-    stores = []
     choose = None
     for n, (b, h) in enumerate(chunks):
         if h == 0:
@@ -187,12 +188,6 @@
         arrived[f, b, :, pl.ds(h * width, width)] = packed[
             b, pl.ds(pl.multiple_of(f * part, part), part), pl.ds(h * width, width)
         ]
-        if h == HALVES - 1:
-            for m, (src, dst) in enumerate([(master_w, master_out), (one_w, one_out), (two_w, two_out)]):
-                cut = pl.ds(b * TILE, TILE)
-                store = pltpu.make_async_copy(src.at[cut, :], dst.at[cut, :], store_sem.at[m * blocks + b])
-                store.start()
-                stores.append(store)
 
     for n, (b, h) in enumerate(chunks):
         for m, copy in row_copies:
@@ -202,17 +197,19 @@
         rollout_w[:, b, :, cut] = (
             rollout_v[:, b, :, cut].astype(jnp.float32) + arrived[:, b, :, cut].astype(jnp.float32)
         ).astype(jnp.bfloat16)
-        if h == HALVES - 1:
-            store = pltpu.make_async_copy(
-                rollout_w.at[:, b], rollout_out.at[:, b], store_sem.at[3 * blocks + b]
-            )
-            store.start()
-            stores.append(store)
 
     for copy in far_copies + near_copies + x_copies + [c for _, c in row_copies]:
         copy.wait_send()
-    for store in stores:
-        store.wait()
+
+
+def write_kernel(*refs):
+    count = len(refs) // 2
+    sem = refs[-1]
+    copies = [pltpu.make_async_copy(refs[n], refs[count + n], sem.at[n]) for n in range(count)]
+    for copy in copies:
+        copy.start()
+    for copy in copies:
+        copy.wait()
 
 
 def fused_body(gradients, master, one, two, synced, rollout, amax, table, shifts):
@@ -222,41 +219,51 @@
     part = TILE // owners
     n = blocks * HALVES
     f32, bf16 = jnp.float32, jnp.bfloat16
-    hbm = pl.BlockSpec(memory_space=pl.ANY)
+    hbm = pl.BlockSpec(memory_space=pltpu.HBM)
     vmem = pl.BlockSpec(memory_space=pltpu.VMEM)
-    smem = pl.BlockSpec(memory_space=pltpu.SMEM)
     grouped = (owners, blocks, part, cols)
     whole = (rows, cols)
     dma = pltpu.SemaphoreType.DMA
+    results = (
+        jax.ShapeDtypeStruct(whole, f32),
+        jax.ShapeDtypeStruct(whole, f32),
+        jax.ShapeDtypeStruct(whole, f32),
+        jax.ShapeDtypeStruct(amax.shape, f32),
+        jax.ShapeDtypeStruct(grouped, bf16),
+    )
     outs = pl.pallas_call(
         functools.partial(fused_kernel, owners),
-        out_shape=(
-            jax.ShapeDtypeStruct(whole, f32),
-            jax.ShapeDtypeStruct(whole, f32),
-            jax.ShapeDtypeStruct(whole, f32),
-            jax.ShapeDtypeStruct(amax.shape, f32),
-            jax.ShapeDtypeStruct(grouped, bf16),
-        ),
-        in_specs=[hbm] * 6 + [smem, vmem, smem],
-        out_specs=(hbm, hbm, hbm, vmem, hbm),
+        out_shape=tuple(pltpu.VMEM(r.shape, r.dtype) for r in results),
+        in_specs=[hbm] * 8 + [pl.BlockSpec(memory_space=pltpu.SMEM)],
+        out_specs=(vmem,) * 5,
         scratch_shapes=(
             [pltpu.VMEM(whole, bf16)] * 6
             + [pltpu.VMEM(whole, f32)] * 3
             + [pltpu.VMEM(whole, bf16), pltpu.VMEM(grouped, bf16)]
-            + [pltpu.VMEM(whole, f32)] * 3
-            + [pltpu.VMEM(grouped, bf16), pltpu.VMEM((blocks, TILE, cols), bf16), pltpu.VMEM(grouped, bf16)]
+            + [pltpu.VMEM((blocks, TILE, cols), bf16), pltpu.VMEM(grouped, bf16)]
+            + [pltpu.SMEM(amax.shape, f32), pltpu.VMEM((1, TILE), jnp.int32)]
             + [
-                dma((7,)), dma((n,)), dma((n,)), dma((blocks,)), dma((blocks,)), dma((n,)), dma((n,)),
-                dma((n, owners - 1)), dma((n, owners - 1)), dma((4 * blocks,)),
+                dma((9,)), dma((n,)), dma((n,)), dma((blocks,)), dma((blocks,)), dma((n,)), dma((n,)),
+                dma((n, owners - 1)), dma((n, owners - 1)),
             ]
         ),
         compiler_params=pltpu.CompilerParams(
             collective_id=0, has_side_effects=True, vmem_limit_bytes=32 * 1024 * 1024
         ),
-    )(
-        gradients[0], master, one, two, synced, rollout.reshape(grouped), amax,
-        table.reshape(1, TILE), shifts,
-    )
+    )(*[
+        pltpu.with_memory_space_constraint(x, pltpu.HBM)
+        for x in (
+            gradients[0], master, one, two, synced, rollout.reshape(grouped), amax,
+            table.reshape(1, TILE),
+        )
+    ], shifts)
+    outs = pl.pallas_call(
+        write_kernel,
+        out_shape=results,
+        in_specs=[vmem] * 5,
+        out_specs=(hbm,) * 5,
+        scratch_shapes=[dma((5,))],
+    )(*outs)
     return outs[0], outs[1], outs[2], outs[3], outs[4].reshape(whole)
 
 

time: 37 us -> 31.3 us (0.85)
  local copies, waits for them, and re-layouts: 12.1 us -> 4 us
  Pallas kernels: 23.3 us -> 25.9 us
    unnamed x21 -> x10, local copies, waits for them, and re-layouts: 12.1 us -> 4 us
    pallas_call x1 -> x2, Pallas kernels: 23.3 us -> 25.9 us  [the longest x1 22.6 us: fused_body(): pl.pallas_call(functools.partial(fused_kernel, owners), out_shape=tuple((...]
where the time goes in v2:
time: 31.3 us; the launch traced here: 31.2 us
  Pallas kernels  25.9 us (83%)
  local copies, waits for them, and re-layouts  4 us (13%)
  between operations  1.3 us (4%)
    pallas_call x1, Pallas kernels, fused_body(): pl.pallas_call(functools.partial(fused_kernel, owners), out_shape=tuple((...  22.6 us
    unnamed x10, local copies, waits for them, and re-layouts  4 us
    pallas_call x1, Pallas kernels, fused_body(): pl.pallas_call(write_kernel, out_shape=results, in_specs=[vmem] * 5, out_...  3.28 us

profile of v2, /device:TPU:0, one launch (start us, length us, event | category | flops | bytes accessed | tf_op | source)
XLA Modules:
  0.0 31.2 jit_solution(17717164498947909287)
XLA Ops:
  1.3 22.6 %shard_map.128 = (f32[384,512]{1,0:T(8,128)S(1)}, f32[384,512]{1,0:T(8,128)S(1)}, f32[384,512]{1,0:T(8,128)S(1)}, f32[3,4]{1,0:T(4,128)S(1)}, bf16[8,3,16,512]{3,2,1,0:T(8,128)(2,1)S(1)}) custom-call(bf16[384,2048]{1,0:T(8,128)(2,1)} %bitcast.4, f32[384,512]{1,0:T(8,128)} %master.1, f32[384,512]{1,0:T(8,128)} %one.1, f32[384,512]{1,0:T(8,128)} %two.1, ...), custom_call_target="tpu_custom_call" | custom-call | tf_op jit(solution)/shard_map/pallas_call | solution.py:234
  23.9 0.0 copy-start
  23.9 0.9 %copy-done = f32[384,512]{1,0:T(8,128)} copy-done((f32[384,512]{1,0:T(8,128)}, f32[384,512]{1,0:T(8,128)S(1)}, u32[]{:S(2)}) %copy-start) | copy-done | bytes 786456
  24.8 0.0 copy-start.1
  24.8 0.9 %copy-done.1 = f32[384,512]{1,0:T(8,128)} copy-done((f32[384,512]{1,0:T(8,128)}, f32[384,512]{1,0:T(8,128)S(1)}, u32[]{:S(2)}) %copy-start.1) | copy-done | bytes 786456
  25.7 0.0 copy-start.2
  25.7 0.9 %copy-done.2 = f32[384,512]{1,0:T(8,128)} copy-done((f32[384,512]{1,0:T(8,128)}, f32[384,512]{1,0:T(8,128)S(1)}, u32[]{:S(2)}) %copy-start.2) | copy-done | bytes 786456
  26.6 0.0 copy-start.3
  26.6 0.7 %copy-done.3 = bf16[8,3,16,512]{3,2,1,0:T(8,128)(2,1)} copy-done((bf16[8,3,16,512]{3,2,1,0:T(8,128)(2,1)}, bf16[8,3,16,512]{3,2,1,0:T(8,128)(2,1)S(1)}, u32[]{:S(2)}) %copy-start.3) | copy-done | bytes 393240
  27.3 0.0 copy-start.4
  27.3 0.6 %copy-done.4 = f32[3,4]{1,0:T(4,128)} copy-done((f32[3,4]{1,0:T(4,128)}, f32[3,4]{1,0:T(4,128)S(1)}, u32[]{:S(2)}) %copy-start.4) | copy-done | bytes 72
  27.9 3.3 %shard_map.129 = (f32[384,512]{1,0:T(8,128)}, f32[384,512]{1,0:T(8,128)}, f32[384,512]{1,0:T(8,128)}, f32[3,4]{1,0:T(4,128)}, bf16[8,3,16,512]{3,2,1,0:T(8,128)(2,1)}) custom-call(f32[384,512]{1,0:T(8,128)} %copy-done, f32[384,512]{1,0:T(8,128)} %copy-done.1, f32[384,512]{1,0:T(8,128)} %copy-done.2, f32[3,4]{1,0:T(4,128)} %copy-done.4, ...), custom_call_target="tpu_custom_call" | custom-call | tf_op jit(solution)/shard_map/pallas_call | solution.py:260
Async XLA Ops:
  23.9 0.9 %copy-start = (f32[384,512]{1,0:T(8,128)}, f32[384,512]{1,0:T(8,128)S(1)}, u32[]{:S(2)}) copy-start(f32[384,512]{1,0:T(8,128)S(1)} %get-tuple-element.15.refs_0_) | copy-start | bytes 2359300
  24.8 0.9 %copy-start.1 = (f32[384,512]{1,0:T(8,128)}, f32[384,512]{1,0:T(8,128)S(1)}, u32[]{:S(2)}) copy-start(f32[384,512]{1,0:T(8,128)S(1)} %get-tuple-element.16.refs_1_) | copy-start | bytes 2359300
  25.7 0.9 %copy-start.2 = (f32[384,512]{1,0:T(8,128)}, f32[384,512]{1,0:T(8,128)S(1)}, u32[]{:S(2)}) copy-start(f32[384,512]{1,0:T(8,128)S(1)} %get-tuple-element.17.refs_2_) | copy-start | bytes 2359300
  26.6 0.7 %copy-start.3 = (bf16[8,3,16,512]{3,2,1,0:T(8,128)(2,1)}, bf16[8,3,16,512]{3,2,1,0:T(8,128)(2,1)S(1)}, u32[]{:S(2)}) copy-start(bf16[8,3,16,512]{3,2,1,0:T(8,128)(2,1)S(1)} %get-tuple-element.19.refs_4_) | copy-start | bytes 1179652
  27.3 0.6 %copy-start.4 = (f32[3,4]{1,0:T(4,128)}, f32[3,4]{1,0:T(4,128)S(1)}, u32[]{:S(2)}) copy-start(f32[3,4]{1,0:T(4,128)S(1)} %get-tuple-element.18.refs_3_) | copy-start | bytes 148

commit v3 on v2

--- a/solution.py
+++ b/solution.py
@@ -83,8 +83,9 @@
             (rollout, rollout_v),
         ])
     ]
-    for load in loads:
+    for load in loads[:4]:
         load.start()
+
     def chooser(b):
         shift = shifts[((f * blocks + b) * TILE) // D]
         dest = (rank + shift * part) & (TILE - 1)
@@ -116,6 +117,9 @@
         )
         copy.start()
         near_copies.append(copy)
+
+    for load in loads[4:]:
+        load.start()
 
     x_copies = []
     loads[2].wait()
@@ -263,7 +267,8 @@
         in_specs=[vmem] * 5,
         out_specs=(hbm,) * 5,
         scratch_shapes=[dma((5,))],
-    )(*outs)
+        compiler_params=pltpu.CompilerParams(vmem_limit_bytes=4 * 1024 * 1024),
+    )(*[pltpu.with_memory_space_constraint(x, pltpu.VMEM) for x in outs])
     return outs[0], outs[1], outs[2], outs[3], outs[4].reshape(whole)
 
 

time: 31.3 us -> 25.6 us (0.82)
  local copies, waits for them, and re-layouts: 4 us -> 0 us
  Pallas kernels: 25.9 us -> 24.2 us
    unnamed x10 -> x0, local copies, waits for them, and re-layouts: 4 us -> none
    pallas_call x1, Pallas kernels: 3.28 us -> 1.57 us  [fused_body(): pl.pallas_call(write_kernel, out_shape=results, in_specs=[vmem] * 5, out_...]
where the time goes in v3:
time: 25.6 us; the launch traced here: 25.5 us
  Pallas kernels  24.2 us (95%)
  between operations  1.29 us (5%)
    pallas_call x1, Pallas kernels, fused_body(): pl.pallas_call(functools.partial(fused_kernel, owners), out_shape=tuple((...  22.6 us
    pallas_call x1, Pallas kernels, fused_body(): pl.pallas_call(write_kernel, out_shape=results, in_specs=[vmem] * 5, out_...  1.57 us

profile of v3, /device:TPU:0, one launch (start us, length us, event | category | flops | bytes accessed | tf_op | source)
XLA Modules:
  0.0 25.5 jit_solution(9684099035236112299)
XLA Ops:
  1.3 22.6 %shard_map.128 = (f32[384,512]{1,0:T(8,128)S(1)}, f32[384,512]{1,0:T(8,128)S(1)}, f32[384,512]{1,0:T(8,128)S(1)}, f32[3,4]{1,0:T(4,128)S(1)}, bf16[8,3,16,512]{3,2,1,0:T(8,128)(2,1)S(1)}) custom-call(bf16[384,2048]{1,0:T(8,128)(2,1)} %bitcast.4, f32[384,512]{1,0:T(8,128)} %master.1, f32[384,512]{1,0:T(8,128)} %one.1, f32[384,512]{1,0:T(8,128)} %two.1, ...), custom_call_target="tpu_custom_call" | custom-call | tf_op jit(solution)/shard_map/pallas_call | solution.py:238
  23.9 1.6 %shard_map.129 = (f32[384,512]{1,0:T(8,128)}, f32[384,512]{1,0:T(8,128)}, f32[384,512]{1,0:T(8,128)}, f32[3,4]{1,0:T(4,128)}, bf16[8,3,16,512]{3,2,1,0:T(8,128)(2,1)}) custom-call(f32[384,512]{1,0:T(8,128)S(1)} %get-tuple-element.15.refs_0_, f32[384,512]{1,0:T(8,128)S(1)} %get-tuple-element.16.refs_1_, f32[384,512]{1,0:T(8,128)S(1)} %get-tuple-element.17.refs_2_, ...), custom_call_target="tpu_custom_call" | custom-call | tf_op jit(solution)/shard_map/pallas_call | solution.py:264

commit v4 on v3

--- a/solution.py
+++ b/solution.py
@@ -29,7 +29,7 @@
     return (new_master, new_one, new_two)
 
 
-HALVES = 2
+SPLIT = 4
 
 
 def flipped(index, mask):
@@ -42,20 +42,28 @@
     return out
 
 
+def adam_fast(master, moment_one, moment_two, summed, replicas):
+    new_one = beta_one * moment_one + ((1.0 - beta_one) / replicas) * summed
+    new_two = beta_two * moment_two + ((1.0 - beta_two) / replicas**2) * (summed * summed)
+    root = jnp.sqrt(new_two * (1.0 / bias_two)) + adam_floor
+    new_master = (1.0 - step_size * weight_decay) * master - (step_size / bias_one) * new_one / root
+    return (new_master, new_one, new_two)
+
+
 def fused_kernel(
     owners, grads, master, one, two, synced, rollout, amax_h, table_h, shifts,
     master_w, one_w, two_w, amax_out, rollout_w,
     far_own, near_own, far_sib, near_sib, far_sum, far_in,
-    master_v, one_v, two_v, synced_v, rollout_v, packed, arrived, amax, table,
+    master_v, one_v, two_v, synced_v, rollout_v, packed, arrived, amax, table, peaks,
     load_sem, far_send, far_recv, near_send, near_recv, x_send, x_recv, row_send, row_recv,
 ):
     d = lax.axis_index("dp")
     f = lax.axis_index("fsdp")
     rows, cols = master_v.shape
     blocks = rows // TILE
-    width = cols // HALVES
+    width = cols // SPLIT
     part = TILE // owners
-    chunks = [(b, h) for b in range(blocks) for h in range(HALVES)]
+    chunks = [(b, h) for b in range(blocks) for h in range(SPLIT)]
     sib = flipped(d, 1)
     opp = flipped(d, 2)
     opp_sib = flipped(d, 3)
@@ -148,7 +156,7 @@
     for load in loads[3:]:
         load.wait()
 
-    row_copies = []
+    targets = [flipped(f, j) for j in sorted(range(1, owners), key=lambda j: -(j // 2))]
     choose = None
     for n, (b, h) in enumerate(chunks):
         if h == 0:
@@ -160,8 +168,8 @@
             + at(near_sib, b, h)[...].astype(jnp.float32)
             + at(far_in, b, h)[...].astype(jnp.float32)
         )
-        new_master, new_one, new_two = adam_step(
-            at(master_v, b, h)[...], at(one_v, b, h)[...], at(two_v, b, h)[...], summed / 4.0
+        new_master, new_one, new_two = adam_fast(
+            at(master_v, b, h)[...], at(one_v, b, h)[...], at(two_v, b, h)[...], summed, 4
         )
         at(master_w, b, h)[...] = new_master
         at(one_w, b, h)[...] = new_one
@@ -171,39 +179,42 @@
         for k in range(width // TILE):
             t = h * (width // TILE) + k
             piece = delta[:, k * TILE : (k + 1) * TILE]
-            top = jnp.max(jnp.max(jnp.abs(piece), axis=0, keepdims=True), axis=1, keepdims=True)
-            amax_out[b : b + 1, t : t + 1] = top
+            peaks[b, t] = jnp.max(jnp.abs(piece).reshape(TILE // 8, 8, TILE), axis=0)
             limit = amax[b, t] / code_limit * code_limit
             restored.append(jnp.clip(piece, -limit, limit).astype(jnp.bfloat16))
         restored = jnp.concatenate(restored, axis=1)
         packed[b, :, pl.ds(h * width, width)] = jnp.dot(
             choose, restored, preferred_element_type=jnp.float32
         ).astype(jnp.bfloat16)
-        for j in sorted(range(1, owners), key=lambda j: -(j // 2)):
-            target = flipped(f, j)
-            copy = pltpu.make_async_remote_copy(
+        for target in targets:
+            pltpu.make_async_remote_copy(
                 src_ref=packed.at[b, pl.ds(pl.multiple_of(target * part, part), part), pl.ds(h * width, width)],
                 dst_ref=arrived.at[f, b, :, pl.ds(h * width, width)],
-                send_sem=row_send.at[n, j - 1], recv_sem=row_recv.at[n, j - 1],
+                send_sem=row_send.at[n], recv_sem=row_recv.at[n],
                 device_id={"fsdp": target}, device_id_type=MESH,
-            )
-            copy.start()
-            row_copies.append((n, copy))
+            ).start()
         arrived[f, b, :, pl.ds(h * width, width)] = packed[
             b, pl.ds(pl.multiple_of(f * part, part), part), pl.ds(h * width, width)
         ]
 
-    for n, (b, h) in enumerate(chunks):
-        for m, copy in row_copies:
-            if m == n:
-                copy.wait_recv()
+    for b in range(blocks):
+        for t in range(cols // TILE):
+            top = jnp.max(jnp.max(peaks[b, t], axis=0, keepdims=True), axis=1, keepdims=True)
+            amax_out[b : b + 1, t : t + 1] = top
+
+    for n, (b, h) in enumerate(chunks):
         cut = pl.ds(h * width, width)
+        others = arrived.at[pl.ds(0, owners - 1), b, :, cut]
+        pltpu.make_async_copy(others, others, row_recv.at[n]).wait()
         rollout_w[:, b, :, cut] = (
             rollout_v[:, b, :, cut].astype(jnp.float32) + arrived[:, b, :, cut].astype(jnp.float32)
         ).astype(jnp.bfloat16)
 
-    for copy in far_copies + near_copies + x_copies + [c for _, c in row_copies]:
+    for copy in far_copies + near_copies + x_copies:
         copy.wait_send()
+    for n, (b, h) in enumerate(chunks):
+        others = arrived.at[pl.ds(0, owners - 1), b, :, pl.ds(h * width, width)]
+        pltpu.make_async_copy(others, others, row_send.at[n]).wait()
 
 
 def write_kernel(*refs):
@@ -221,7 +232,7 @@
     rows, cols = master.shape
     blocks = rows // TILE
     part = TILE // owners
-    n = blocks * HALVES
+    n = blocks * SPLIT
     f32, bf16 = jnp.float32, jnp.bfloat16
     hbm = pl.BlockSpec(memory_space=pltpu.HBM)
     vmem = pl.BlockSpec(memory_space=pltpu.VMEM)
@@ -246,9 +257,10 @@
             + [pltpu.VMEM(whole, bf16), pltpu.VMEM(grouped, bf16)]
             + [pltpu.VMEM((blocks, TILE, cols), bf16), pltpu.VMEM(grouped, bf16)]
             + [pltpu.SMEM(amax.shape, f32), pltpu.VMEM((1, TILE), jnp.int32)]
+            + [pltpu.VMEM((blocks, cols // TILE, 8, TILE), f32)]
             + [
                 dma((9,)), dma((n,)), dma((n,)), dma((blocks,)), dma((blocks,)), dma((n,)), dma((n,)),
-                dma((n, owners - 1)), dma((n, owners - 1)),
+                dma((n,)), dma((n,)),
             ]
         ),
         compiler_params=pltpu.CompilerParams(

time: 25.6 us -> 24.5 us (0.957)
  Pallas kernels: 24.2 us -> 23.1 us
    pallas_call x1, Pallas kernels: 22.6 us -> 21.5 us  [fused_body(): pl.pallas_call(functools.partial(fused_kernel, owners), out_shape=tuple((...]
where the time goes in v4:
time: 24.5 us; the launch traced here: 24.3 us
  Pallas kernels  23.1 us (94%)
  between operations  1.29 us (5%)
    pallas_call x1, Pallas kernels, fused_body(): pl.pallas_call(functools.partial(fused_kernel, owners), out_shape=tuple((...  21.5 us
    pallas_call x1, Pallas kernels, fused_body(): pl.pallas_call(write_kernel, out_shape=results, in_specs=[vmem] * 5, out_...  1.57 us

profile of v4, /device:TPU:0, one launch (start us, length us, event | category | flops | bytes accessed | tf_op | source)
XLA Modules:
  0.0 24.3 jit_solution(12210578515727437561)
XLA Ops:
  1.3 21.5 %shard_map.128 = (f32[384,512]{1,0:T(8,128)S(1)}, f32[384,512]{1,0:T(8,128)S(1)}, f32[384,512]{1,0:T(8,128)S(1)}, f32[3,4]{1,0:T(4,128)S(1)}, bf16[8,3,16,512]{3,2,1,0:T(8,128)(2,1)S(1)}) custom-call(bf16[384,2048]{1,0:T(8,128)(2,1)} %bitcast.4, f32[384,512]{1,0:T(8,128)} %master.1, f32[384,512]{1,0:T(8,128)} %one.1, f32[384,512]{1,0:T(8,128)} %two.1, ...), custom_call_target="tpu_custom_call" | custom-call | tf_op jit(solution)/shard_map/pallas_call | solution.py:249
  22.8 1.6 %shard_map.129 = (f32[384,512]{1,0:T(8,128)}, f32[384,512]{1,0:T(8,128)}, f32[384,512]{1,0:T(8,128)}, f32[3,4]{1,0:T(4,128)}, bf16[8,3,16,512]{3,2,1,0:T(8,128)(2,1)}) custom-call(f32[384,512]{1,0:T(8,128)S(1)} %get-tuple-element.15.refs_0_, f32[384,512]{1,0:T(8,128)S(1)} %get-tuple-element.16.refs_1_, f32[384,512]{1,0:T(8,128)S(1)} %get-tuple-element.17.refs_2_, ...), custom_call_target="tpu_custom_call" | custom-call | tf_op jit(solution)/shard_map/pallas_call | solution.py:276

commit v5 on v4

--- a/solution.py
+++ b/solution.py
@@ -30,6 +30,7 @@
 
 
 SPLIT = 4
+WINDOW = 3
 
 
 def flipped(index, mask):
@@ -127,11 +128,13 @@
         near_copies.append(copy)
 
     for load in loads[4:]:
-        load.start()
+        load.start(priority=1)
 
     x_copies = []
     loads[2].wait()
-    for n, (b, h) in enumerate(chunks):
+
+    def send_x(n):
+        b, h = chunks[n]
         far_copies[n].wait_recv()
         mine = at(far_own, b, h)[...].astype(jnp.float32)
         theirs = at(far_sib, b, h)[...].astype(jnp.float32)
@@ -144,6 +147,9 @@
         copy.start()
         x_copies.append(copy)
 
+    for n in range(WINDOW):
+        send_x(n)
+
     for load in loads[:2]:
         load.wait()
 
@@ -162,6 +168,8 @@
         if h == 0:
             near_copies[b].wait_recv()
             choose = chooser(b)
+        if n + WINDOW < len(chunks):
+            send_x(n + WINDOW)
         x_copies[n].wait_recv()
         summed = (
             at(near_own, b, h)[...].astype(jnp.float32)

time: 24.5 us -> 25.4 us (1.037)
  Pallas kernels: 23.1 us -> 23.9 us
    pallas_call x1, Pallas kernels: 21.5 us -> 22.3 us  [fused_body(): pl.pallas_call(functools.partial(fused_kernel, owners), out_shape=tuple((...]
where the time goes in v5:
time: 25.4 us; the launch traced here: 25.2 us
  Pallas kernels  23.9 us (94%)
  between operations  1.29 us (5%)
    pallas_call x1, Pallas kernels, fused_body(): pl.pallas_call(functools.partial(fused_kernel, owners), out_shape=tuple((...  22.3 us
    pallas_call x1, Pallas kernels, fused_body(): pl.pallas_call(write_kernel, out_shape=results, in_specs=[vmem] * 5, out_...  1.57 us

profile of v5, /device:TPU:0, one launch (start us, length us, event | category | flops | bytes accessed | tf_op | source)
XLA Modules:
  0.0 25.2 jit_solution(1508400257655966514)
XLA Ops:
  1.3 22.3 %shard_map.128 = (f32[384,512]{1,0:T(8,128)S(1)}, f32[384,512]{1,0:T(8,128)S(1)}, f32[384,512]{1,0:T(8,128)S(1)}, f32[3,4]{1,0:T(4,128)S(1)}, bf16[8,3,16,512]{3,2,1,0:T(8,128)(2,1)S(1)}) custom-call(bf16[384,2048]{1,0:T(8,128)(2,1)} %bitcast.4, f32[384,512]{1,0:T(8,128)} %master.1, f32[384,512]{1,0:T(8,128)} %one.1, f32[384,512]{1,0:T(8,128)} %two.1, ...), custom_call_target="tpu_custom_call" | custom-call | tf_op jit(solution)/shard_map/pallas_call | solution.py:257
  23.6 1.6 %shard_map.129 = (f32[384,512]{1,0:T(8,128)}, f32[384,512]{1,0:T(8,128)}, f32[384,512]{1,0:T(8,128)}, f32[3,4]{1,0:T(4,128)}, bf16[8,3,16,512]{3,2,1,0:T(8,128)(2,1)}) custom-call(f32[384,512]{1,0:T(8,128)S(1)} %get-tuple-element.15.refs_0_, f32[384,512]{1,0:T(8,128)S(1)} %get-tuple-element.16.refs_1_, f32[384,512]{1,0:T(8,128)S(1)} %get-tuple-element.17.refs_2_, ...), custom_call_target="tpu_custom_call" | custom-call | tf_op jit(solution)/shard_map/pallas_call | solution.py:284

commit v6 on v4

--- a/solution.py
+++ b/solution.py
@@ -29,7 +29,7 @@
     return (new_master, new_one, new_two)
 
 
-SPLIT = 4
+SPLIT = 2
 
 
 def flipped(index, mask):

time: 24.5 us -> 24.9 us (1.016)
  Pallas kernels: 23.1 us -> 23.4 us
    pallas_call x1, Pallas kernels: 21.5 us -> 21.9 us  [fused_body(): pl.pallas_call(functools.partial(fused_kernel, owners), out_shape=tuple((...]
where the time goes in v6:
time: 24.9 us; the launch traced here: 24.7 us
  Pallas kernels  23.4 us (94%)
  between operations  1.29 us (5%)
    pallas_call x1, Pallas kernels, fused_body(): pl.pallas_call(functools.partial(fused_kernel, owners), out_shape=tuple((...  21.9 us
    pallas_call x1, Pallas kernels, fused_body(): pl.pallas_call(write_kernel, out_shape=results, in_specs=[vmem] * 5, out_...  1.57 us

profile of v6, /device:TPU:0, one launch (start us, length us, event | category | flops | bytes accessed | tf_op | source)
XLA Modules:
  0.0 24.7 jit_solution(9807177591541664816)
XLA Ops:
  1.3 21.9 %shard_map.128 = (f32[384,512]{1,0:T(8,128)S(1)}, f32[384,512]{1,0:T(8,128)S(1)}, f32[384,512]{1,0:T(8,128)S(1)}, f32[3,4]{1,0:T(4,128)S(1)}, bf16[8,3,16,512]{3,2,1,0:T(8,128)(2,1)S(1)}) custom-call(bf16[384,2048]{1,0:T(8,128)(2,1)} %bitcast.4, f32[384,512]{1,0:T(8,128)} %master.1, f32[384,512]{1,0:T(8,128)} %one.1, f32[384,512]{1,0:T(8,128)} %two.1, ...), custom_call_target="tpu_custom_call" | custom-call | tf_op jit(solution)/shard_map/pallas_call | solution.py:249
  23.2 1.6 %shard_map.129 = (f32[384,512]{1,0:T(8,128)}, f32[384,512]{1,0:T(8,128)}, f32[384,512]{1,0:T(8,128)}, f32[3,4]{1,0:T(4,128)}, bf16[8,3,16,512]{3,2,1,0:T(8,128)(2,1)}) custom-call(f32[384,512]{1,0:T(8,128)S(1)} %get-tuple-element.15.refs_0_, f32[384,512]{1,0:T(8,128)S(1)} %get-tuple-element.16.refs_1_, f32[384,512]{1,0:T(8,128)S(1)} %get-tuple-element.17.refs_2_, ...), custom_call_target="tpu_custom_call" | custom-call | tf_op jit(solution)/shard_map/pallas_call | solution.py:276

commit v7 on v6

--- a/solution.py
+++ b/solution.py
@@ -29,7 +29,21 @@
     return (new_master, new_one, new_two)
 
 
-SPLIT = 2
+def chunks_of(blocks, cols):
+    out = []
+    for b in range(blocks):
+        thin = cols // 2 if cols // 2 % TILE == 0 else cols
+        widths = [thin] * (cols // thin)
+        if thin % (2 * TILE) == 0:
+            if b == 0:
+                widths[:1] = [thin // 2] * 2
+            if b == blocks - 1:
+                widths[-1:] = [thin // 2] * 2
+        start = 0
+        for width in widths:
+            out.append((b, start, width))
+            start += width
+    return out
 
 
 def flipped(index, mask):
@@ -61,9 +75,8 @@
     f = lax.axis_index("fsdp")
     rows, cols = master_v.shape
     blocks = rows // TILE
-    width = cols // SPLIT
     part = TILE // owners
-    chunks = [(b, h) for b in range(blocks) for h in range(SPLIT)]
+    chunks = chunks_of(blocks, cols)
     sib = flipped(d, 1)
     opp = flipped(d, 2)
     opp_sib = flipped(d, 3)
@@ -101,15 +114,15 @@
 
     pl.semaphore_wait(barrier, owners + 1)
 
-    def at(ref, b, h):
-        return ref.at[pl.ds(b * TILE, TILE), pl.ds(h * width, width)]
+    def at(ref, b, c, width):
+        return ref.at[pl.ds(b * TILE, TILE), pl.ds(c, width)]
 
     far_copies = []
-    for n, (b, h) in enumerate(chunks):
-        source = pl.multiple_of(opp_sib * cols + h * width, width)
+    for n, (b, c, width) in enumerate(chunks):
+        source = pl.multiple_of(opp_sib * cols + c, TILE)
         copy = pltpu.make_async_remote_copy(
             src_ref=grads.at[pl.ds(b * TILE, TILE), pl.ds(source, width)],
-            dst_ref=at(far_sib, b, h),
+            dst_ref=at(far_sib, b, c, width),
             send_sem=far_send.at[n], recv_sem=far_recv.at[n],
             device_id={"dp": sib}, device_id_type=MESH,
         )
@@ -131,13 +144,13 @@
 
     x_copies = []
     loads[2].wait()
-    for n, (b, h) in enumerate(chunks):
+    for n, (b, c, width) in enumerate(chunks):
         far_copies[n].wait_recv()
-        mine = at(far_own, b, h)[...].astype(jnp.float32)
-        theirs = at(far_sib, b, h)[...].astype(jnp.float32)
-        at(far_sum, b, h)[...] = (mine + theirs).astype(jnp.bfloat16)
+        mine = at(far_own, b, c, width)[...].astype(jnp.float32)
+        theirs = at(far_sib, b, c, width)[...].astype(jnp.float32)
+        at(far_sum, b, c, width)[...] = (mine + theirs).astype(jnp.bfloat16)
         copy = pltpu.make_async_remote_copy(
-            src_ref=at(far_sum, b, h), dst_ref=at(far_in, b, h),
+            src_ref=at(far_sum, b, c, width), dst_ref=at(far_in, b, c, width),
             send_sem=x_send.at[n], recv_sem=x_recv.at[n],
             device_id={"dp": opp}, device_id_type=MESH,
         )
@@ -158,43 +171,43 @@
 
     targets = [flipped(f, j) for j in sorted(range(1, owners), key=lambda j: -(j // 2))]
     choose = None
-    for n, (b, h) in enumerate(chunks):
-        if h == 0:
+    for n, (b, c, width) in enumerate(chunks):
+        if c == 0:
             near_copies[b].wait_recv()
             choose = chooser(b)
         x_copies[n].wait_recv()
         summed = (
-            at(near_own, b, h)[...].astype(jnp.float32)
-            + at(near_sib, b, h)[...].astype(jnp.float32)
-            + at(far_in, b, h)[...].astype(jnp.float32)
+            at(near_own, b, c, width)[...].astype(jnp.float32)
+            + at(near_sib, b, c, width)[...].astype(jnp.float32)
+            + at(far_in, b, c, width)[...].astype(jnp.float32)
         )
         new_master, new_one, new_two = adam_fast(
-            at(master_v, b, h)[...], at(one_v, b, h)[...], at(two_v, b, h)[...], summed, 4
-        )
-        at(master_w, b, h)[...] = new_master
-        at(one_w, b, h)[...] = new_one
-        at(two_w, b, h)[...] = new_two
-        delta = new_master - at(synced_v, b, h)[...].astype(jnp.float32)
+            at(master_v, b, c, width)[...], at(one_v, b, c, width)[...], at(two_v, b, c, width)[...], summed, 4
+        )
+        at(master_w, b, c, width)[...] = new_master
+        at(one_w, b, c, width)[...] = new_one
+        at(two_w, b, c, width)[...] = new_two
+        delta = new_master - at(synced_v, b, c, width)[...].astype(jnp.float32)
         restored = []
         for k in range(width // TILE):
-            t = h * (width // TILE) + k
+            t = c // TILE + k
             piece = delta[:, k * TILE : (k + 1) * TILE]
             peaks[b, t] = jnp.max(jnp.abs(piece).reshape(TILE // 8, 8, TILE), axis=0)
             limit = amax[b, t] / code_limit * code_limit
             restored.append(jnp.clip(piece, -limit, limit).astype(jnp.bfloat16))
         restored = jnp.concatenate(restored, axis=1)
-        packed[b, :, pl.ds(h * width, width)] = jnp.dot(
+        packed[b, :, pl.ds(c, width)] = jnp.dot(
             choose, restored, preferred_element_type=jnp.float32
         ).astype(jnp.bfloat16)
         for target in targets:
             pltpu.make_async_remote_copy(
-                src_ref=packed.at[b, pl.ds(pl.multiple_of(target * part, part), part), pl.ds(h * width, width)],
-                dst_ref=arrived.at[f, b, :, pl.ds(h * width, width)],
+                src_ref=packed.at[b, pl.ds(pl.multiple_of(target * part, part), part), pl.ds(c, width)],
+                dst_ref=arrived.at[f, b, :, pl.ds(c, width)],
                 send_sem=row_send.at[n], recv_sem=row_recv.at[n],
                 device_id={"fsdp": target}, device_id_type=MESH,
             ).start()
-        arrived[f, b, :, pl.ds(h * width, width)] = packed[
-            b, pl.ds(pl.multiple_of(f * part, part), part), pl.ds(h * width, width)
+        arrived[f, b, :, pl.ds(c, width)] = packed[
+            b, pl.ds(pl.multiple_of(f * part, part), part), pl.ds(c, width)
         ]
 
     for b in range(blocks):
@@ -202,8 +215,8 @@
             top = jnp.max(jnp.max(peaks[b, t], axis=0, keepdims=True), axis=1, keepdims=True)
             amax_out[b : b + 1, t : t + 1] = top
 
-    for n, (b, h) in enumerate(chunks):
-        cut = pl.ds(h * width, width)
+    for n, (b, c, width) in enumerate(chunks):
+        cut = pl.ds(c, width)
         others = arrived.at[pl.ds(0, owners - 1), b, :, cut]
         pltpu.make_async_copy(others, others, row_recv.at[n]).wait()
         rollout_w[:, b, :, cut] = (
@@ -212,8 +225,8 @@
 
     for copy in far_copies + near_copies + x_copies:
         copy.wait_send()
-    for n, (b, h) in enumerate(chunks):
-        others = arrived.at[pl.ds(0, owners - 1), b, :, pl.ds(h * width, width)]
+    for n, (b, c, width) in enumerate(chunks):
+        others = arrived.at[pl.ds(0, owners - 1), b, :, pl.ds(c, width)]
         pltpu.make_async_copy(others, others, row_send.at[n]).wait()
 
 
@@ -232,7 +245,7 @@
     rows, cols = master.shape
     blocks = rows // TILE
     part = TILE // owners
-    n = blocks * SPLIT
+    n = len(chunks_of(blocks, cols))
     f32, bf16 = jnp.float32, jnp.bfloat16
     hbm = pl.BlockSpec(memory_space=pltpu.HBM)
     vmem = pl.BlockSpec(memory_space=pltpu.VMEM)

time: 24.9 us -> 25 us (level)
  no operation moved by 1% of the time
where the time goes in v7:
time: 25 us; the launch traced here: 24.9 us
  Pallas kernels  23.6 us (94%)
  between operations  1.29 us (5%)
    pallas_call x1, Pallas kernels, fused_body(): pl.pallas_call(functools.partial(fused_kernel, owners), out_shape=tuple((...  22 us
    pallas_call x1, Pallas kernels, fused_body(): pl.pallas_call(write_kernel, out_shape=results, in_specs=[vmem] * 5, out_...  1.57 us

profile of v7, /device:TPU:0, one launch (start us, length us, event | category | flops | bytes accessed | tf_op | source)
XLA Modules:
  0.0 24.9 jit_solution(16601614839916946842)
XLA Ops:
  1.3 22.0 %shard_map.128 = (f32[384,512]{1,0:T(8,128)S(1)}, f32[384,512]{1,0:T(8,128)S(1)}, f32[384,512]{1,0:T(8,128)S(1)}, f32[3,4]{1,0:T(4,128)S(1)}, bf16[8,3,16,512]{3,2,1,0:T(8,128)(2,1)S(1)}) custom-call(bf16[384,2048]{1,0:T(8,128)(2,1)} %bitcast.4, f32[384,512]{1,0:T(8,128)} %master.1, f32[384,512]{1,0:T(8,128)} %one.1, f32[384,512]{1,0:T(8,128)} %two.1, ...), custom_call_target="tpu_custom_call" | custom-call | tf_op jit(solution)/shard_map/pallas_call | solution.py:262
  23.3 1.6 %shard_map.129 = (f32[384,512]{1,0:T(8,128)}, f32[384,512]{1,0:T(8,128)}, f32[384,512]{1,0:T(8,128)}, f32[3,4]{1,0:T(4,128)}, bf16[8,3,16,512]{3,2,1,0:T(8,128)(2,1)}) custom-call(f32[384,512]{1,0:T(8,128)S(1)} %get-tuple-element.15.refs_0_, f32[384,512]{1,0:T(8,128)S(1)} %get-tuple-element.16.refs_1_, f32[384,512]{1,0:T(8,128)S(1)} %get-tuple-element.17.refs_2_, ...), custom_call_target="tpu_custom_call" | custom-call | tf_op jit(solution)/shard_map/pallas_call | solution.py:289

commit v8 on v5

--- a/solution.py
+++ b/solution.py
@@ -30,7 +30,7 @@
 
 
 SPLIT = 4
-WINDOW = 3
+WINDOW = 6
 
 
 def flipped(index, mask):
@@ -117,7 +117,8 @@
         copy.start()
         far_copies.append(copy)
     near_copies = []
-    for b in range(blocks):
+
+    def send_near(b):
         copy = pltpu.make_async_remote_copy(
             src_ref=grads.at[pl.ds(b * TILE, TILE), columns(sib)],
             dst_ref=near_sib.at[pl.ds(b * TILE, TILE), :],
@@ -127,8 +128,9 @@
         copy.start()
         near_copies.append(copy)
 
+    send_near(0)
     for load in loads[4:]:
-        load.start(priority=1)
+        load.start()
 
     x_copies = []
     loads[2].wait()
@@ -149,6 +151,8 @@
 
     for n in range(WINDOW):
         send_x(n)
+    for b in range(1, blocks):
+        send_near(b)
 
     for load in loads[:2]:
         load.wait()

time: 25.4 us -> 24.5 us (0.965)
  Pallas kernels: 23.9 us -> 23.1 us
    pallas_call x1, Pallas kernels: 22.3 us -> 21.5 us  [fused_body(): pl.pallas_call(functools.partial(fused_kernel, owners), out_shape=tuple((...]
where the time goes in v8:
time: 24.5 us; the launch traced here: 24.3 us
  Pallas kernels  23.1 us (94%)
  between operations  1.29 us (5%)
    pallas_call x1, Pallas kernels, fused_body(): pl.pallas_call(functools.partial(fused_kernel, owners), out_shape=tuple((...  21.5 us
    pallas_call x1, Pallas kernels, fused_body(): pl.pallas_call(write_kernel, out_shape=results, in_specs=[vmem] * 5, out_...  1.57 us

profile of v8, /device:TPU:0, one launch (start us, length us, event | category | flops | bytes accessed | tf_op | source)
XLA Modules:
  0.0 24.3 jit_solution(31565859385567180)
XLA Ops:
  1.3 21.5 %shard_map.128 = (f32[384,512]{1,0:T(8,128)S(1)}, f32[384,512]{1,0:T(8,128)S(1)}, f32[384,512]{1,0:T(8,128)S(1)}, f32[3,4]{1,0:T(4,128)S(1)}, bf16[8,3,16,512]{3,2,1,0:T(8,128)(2,1)S(1)}) custom-call(bf16[384,2048]{1,0:T(8,128)(2,1)} %bitcast.4, f32[384,512]{1,0:T(8,128)} %master.1, f32[384,512]{1,0:T(8,128)} %one.1, f32[384,512]{1,0:T(8,128)} %two.1, ...), custom_call_target="tpu_custom_call" | custom-call | tf_op jit(solution)/shard_map/pallas_call | solution.py:261
  22.8 1.6 %shard_map.129 = (f32[384,512]{1,0:T(8,128)}, f32[384,512]{1,0:T(8,128)}, f32[384,512]{1,0:T(8,128)}, f32[3,4]{1,0:T(4,128)}, bf16[8,3,16,512]{3,2,1,0:T(8,128)(2,1)}) custom-call(f32[384,512]{1,0:T(8,128)S(1)} %get-tuple-element.15.refs_0_, f32[384,512]{1,0:T(8,128)S(1)} %get-tuple-element.16.refs_1_, f32[384,512]{1,0:T(8,128)S(1)} %get-tuple-element.17.refs_2_, ...), custom_call_target="tpu_custom_call" | custom-call | tf_op jit(solution)/shard_map/pallas_call | solution.py:288

commit v9 on v8

--- a/solution.py
+++ b/solution.py
@@ -198,7 +198,7 @@
         packed[b, :, pl.ds(h * width, width)] = jnp.dot(
             choose, restored, preferred_element_type=jnp.float32
         ).astype(jnp.bfloat16)
-        for target in targets:
+        for target in targets[:: 1 - 2 * (n % 2)]:
             pltpu.make_async_remote_copy(
                 src_ref=packed.at[b, pl.ds(pl.multiple_of(target * part, part), part), pl.ds(h * width, width)],
                 dst_ref=arrived.at[f, b, :, pl.ds(h * width, width)],

time: 24.5 us -> 24.6 us (level)
  no operation moved by 1% of the time
where the time goes in v9:
time: 24.6 us; the launch traced here: 24.5 us
  Pallas kernels  23.2 us (94%)
  between operations  1.29 us (5%)
    pallas_call x1, Pallas kernels, fused_body(): pl.pallas_call(functools.partial(fused_kernel, owners), out_shape=tuple((...  21.6 us
    pallas_call x1, Pallas kernels, fused_body(): pl.pallas_call(write_kernel, out_shape=results, in_specs=[vmem] * 5, out_...  1.57 us

profile of v9, /device:TPU:0, one launch (start us, length us, event | category | flops | bytes accessed | tf_op | source)
XLA Modules:
  0.0 24.5 jit_solution(8874054061922942546)
XLA Ops:
  1.3 21.6 %shard_map.128 = (f32[384,512]{1,0:T(8,128)S(1)}, f32[384,512]{1,0:T(8,128)S(1)}, f32[384,512]{1,0:T(8,128)S(1)}, f32[3,4]{1,0:T(4,128)S(1)}, bf16[8,3,16,512]{3,2,1,0:T(8,128)(2,1)S(1)}) custom-call(bf16[384,2048]{1,0:T(8,128)(2,1)} %bitcast.4, f32[384,512]{1,0:T(8,128)} %master.1, f32[384,512]{1,0:T(8,128)} %one.1, f32[384,512]{1,0:T(8,128)} %two.1, ...), custom_call_target="tpu_custom_call" | custom-call | tf_op jit(solution)/shard_map/pallas_call | solution.py:261
  22.9 1.6 %shard_map.129 = (f32[384,512]{1,0:T(8,128)}, f32[384,512]{1,0:T(8,128)}, f32[384,512]{1,0:T(8,128)}, f32[3,4]{1,0:T(4,128)}, bf16[8,3,16,512]{3,2,1,0:T(8,128)(2,1)}) custom-call(f32[384,512]{1,0:T(8,128)S(1)} %get-tuple-element.15.refs_0_, f32[384,512]{1,0:T(8,128)S(1)} %get-tuple-element.16.refs_1_, f32[384,512]{1,0:T(8,128)S(1)} %get-tuple-element.17.refs_2_, ...), custom_call_target="tpu_custom_call" | custom-call | tf_op jit(solution)/shard_map/pallas_call | solution.py:288
